TPU v7x, 256 devices: a whole 4x4x8 slice. The times are simulated.
256 devices in a mesh: section: 4 (over x), pack: 32 (over z, y), tensor: 2 (over core).
Axes of the slice: x: 4, y: 4, z: 8, core: 2. Of those that a mesh axis runs over, the one named last changes fastest.
Arguments:
- queries: bfloat16 [4, 16384, 2560], P('section', 'pack', 'tensor')
- keys: bfloat16 [4, 16384, 2560], P('section', 'pack', 'tensor')
- values: bfloat16 [4, 16384, 2560], P('section', 'pack', 'tensor'), may hold values from -6 to 6
- seg_len: int32 [4, 32, 16], replicated, may hold values from 1 to 64, as said below
Outputs:
- context: bfloat16 [4, 16384, 2560], P('section', ('pack', 'tensor'))
Inputs may be any that keep to these rules, and one draw needn't show every extreme that they name: seg_len[m, p] lists in order the lengths of the 16 segments of home p's rows; they sum to 512, and each home has a segment of exactly 64 rows.
All inputs are finite; a program needn't handle non-finite values.
Results may differ from a plain program's by a relative error of at most 0.0049.
Values may be sent and summed in bfloat16 or wider, within the bound.
A program may use at most 128 MiB of HBM per device.

v0:
```python
import math

import jax
import jax.numpy as jnp
from jax import lax
from jax.sharding import PartitionSpec as P

HEAD_DIM = 128


masked_score = -1e30


def passed_along(value, axis, steps):
    count = lax.axis_size(axis)
    pairs = [(source, (source + steps) % count) for source in range(count)]
    return lax.ppermute(value, axis, pairs)


def segment_ids(home_count, seg_count):
    seg_ids = jnp.arange(home_count * seg_count, dtype=jnp.int32).reshape(home_count, seg_count)
    joined = jnp.concatenate([seg_ids[:1, 0], seg_ids[:-1, seg_count - 1]])
    return seg_ids.at[:, 0].set(joined)


def owner_offsets(home_len):
    seg_count = home_len.shape[0]
    seg_range = jnp.arange(seg_count, dtype=jnp.int32)
    middle = (seg_range > 0) & (seg_range < seg_count - 1)
    cost = home_len * home_len
    beats = (cost[None, :] > cost[:, None]) | (cost[None, :] == cost[:, None]) & (
        seg_range[None, :] < seg_range[:, None]
    )
    rank = jnp.sum(jnp.where(beats & middle[None, :], 1, 0), axis=1).astype(jnp.int32)
    return jnp.where(
        seg_range == 0, 0, jnp.where(seg_range == seg_count - 1, seg_count - 1, 1 + rank)
    )


def attend(query_rows, key_pad, value_pad, label_query, label_pad, margin):
    total = query_rows.shape[0]
    block_rows = min(total, max(margin, 512 // margin * margin))
    score_scale = 1.0 / math.sqrt(query_rows.shape[2])

    def one_block(block_index):
        start = block_index * block_rows
        query_block = lax.dynamic_slice_in_dim(query_rows, start, block_rows, 0)
        key_block = lax.dynamic_slice_in_dim(key_pad, start, block_rows + 2 * margin, 0)
        value_block = lax.dynamic_slice_in_dim(value_pad, start, block_rows + 2 * margin, 0)
        label_rows = lax.dynamic_slice_in_dim(label_query, start, block_rows, 0)
        label_keys = lax.dynamic_slice_in_dim(label_pad, start, block_rows + 2 * margin, 0)
        scores = (
            jnp.einsum("qhd,khd->hqk", query_block, key_block, preferred_element_type=jnp.float32)
            * score_scale
        )
        scores = jnp.where((label_rows[:, None] == label_keys[None, :])[None], scores, masked_score)
        row_max = jnp.max(scores, axis=2, keepdims=True)
        weights = jnp.exp(scores - row_max)
        weights = (weights / jnp.sum(weights, axis=2, keepdims=True)).astype(jnp.bfloat16)
        mixed = jnp.einsum("hqk,khd->qhd", weights, value_block, preferred_element_type=jnp.float32)
        return mixed.astype(jnp.bfloat16)

    blocks = lax.map(one_block, jnp.arange(total // block_rows, dtype=jnp.int32))
    return blocks.reshape(query_rows.shape)


def padded_rows(rows_in, margin):
    padding = jnp.zeros((margin,) + rows_in.shape[1:], rows_in.dtype)
    return jnp.concatenate([padding, rows_in, padding])


def per_device(queries, keys, values, seg_len):
    home_count = lax.axis_size("pack")
    home_index = lax.axis_index("pack")
    section_index = lax.axis_index("section")
    query_rows, key_rows, value_rows = (queries[0], keys[0], values[0])
    lengths = lax.dynamic_index_in_dim(seg_len, section_index, 0, keepdims=False)
    row_count, feat_count = query_rows.shape
    seg_count = lengths.shape[1]
    head_count = feat_count // HEAD_DIM
    capacity = 2 * row_count // seg_count
    seg_ids = segment_ids(home_count, seg_count)
    row_shape = (row_count, head_count, HEAD_DIM)
    query_three = query_rows.reshape(row_shape)
    key_three = key_rows.reshape(row_shape)
    value_three = value_rows.reshape(row_shape)
    all_offsets = jax.vmap(owner_offsets)(lengths)
    mine = lax.dynamic_index_in_dim(lengths, home_index, 0, keepdims=False)
    mine_offsets = lax.dynamic_index_in_dim(all_offsets, home_index, 0, keepdims=False)
    mine_ends = jnp.cumsum(mine)
    mine_starts = mine_ends - mine
    seg_range = jnp.arange(seg_count, dtype=jnp.int32)
    home_range = jnp.arange(home_count, dtype=jnp.int32)
    slot_owner = (home_index * (seg_count - 1) + mine_offsets) % home_count
    match = slot_owner[None, :] == home_range[:, None]
    seg_rows = jnp.sum(jnp.where(match, mine[None, :], 0), axis=1)
    seg_start = jnp.sum(jnp.where(match, mine_starts[None, :], 0), axis=1)
    offsets = jnp.arange(capacity, dtype=jnp.int32)
    used = offsets[None, :] < seg_rows[:, None]
    picked = jnp.where(used, seg_start[:, None] + offsets[None, :], 0).reshape(-1)
    slot_shape = (home_count, capacity, head_count, HEAD_DIM)
    send_query = jnp.take(query_three, picked, axis=0).reshape(slot_shape)
    send_key = jnp.take(key_three, picked, axis=0).reshape(slot_shape)
    send_value = jnp.take(value_three, picked, axis=0).reshape(slot_shape)
    sender_offset = (home_index - home_range * (seg_count - 1)) % home_count
    has_seg = sender_offset < seg_count
    chosen = all_offsets == jnp.minimum(sender_offset, seg_count - 1)[:, None]
    recv_rows = jnp.where(has_seg, jnp.sum(jnp.where(chosen, lengths, 0), axis=1), 0)
    recv_ids = jnp.sum(jnp.where(chosen, seg_ids, 0), axis=1)
    recv_labels = jnp.where(offsets[None, :] < recv_rows[:, None], recv_ids[:, None], -1).reshape(
        -1
    )
    label_pad = jnp.concatenate(
        [jnp.full((capacity,), -1, jnp.int32), recv_labels, jnp.full((capacity,), -1, jnp.int32)]
    )

    def slot_rows(arrived):
        return arrived.reshape(home_count * capacity, arrived.shape[2], HEAD_DIM)

    arrived_query, arrived_key, arrived_value = (
        lax.all_to_all(send_query, "pack", split_axis=0, concat_axis=0, tiled=True),
        lax.all_to_all(send_key, "pack", split_axis=0, concat_axis=0, tiled=True),
        lax.all_to_all(send_value, "pack", split_axis=0, concat_axis=0, tiled=True),
    )
    mixed = attend(
        slot_rows(arrived_query),
        padded_rows(slot_rows(arrived_key), capacity),
        padded_rows(slot_rows(arrived_value), capacity),
        recv_labels,
        label_pad,
        capacity,
    )
    returned = lax.all_to_all(
        mixed.reshape(slot_shape), "pack", split_axis=0, concat_axis=0, tiled=True
    )
    row_range = jnp.arange(row_count, dtype=jnp.int32)
    row_seg = jnp.sum((row_range[:, None] >= mine_ends[None, :]).astype(jnp.int32), axis=1)
    row_match = row_seg[:, None] == seg_range[None, :]
    row_owner = jnp.sum(jnp.where(row_match, slot_owner[None, :], 0), axis=1)
    row_start = jnp.sum(jnp.where(row_match, mine_starts[None, :], 0), axis=1)
    flat_index = row_owner * capacity + row_range - row_start
    home_rows = jnp.take(
        returned.reshape(home_count * capacity, head_count, HEAD_DIM), flat_index, axis=0
    )
    split_rows = lax.all_to_all(
        home_rows.reshape(row_count, feat_count), "tensor", split_axis=0, concat_axis=1, tiled=True
    )
    handed = passed_along(split_rows, "section", 1)
    return handed[None]


def solution(mesh):
    return jax.shard_map(
        per_device,
        mesh=mesh,
        in_specs=(
            P("section", "pack", "tensor"),
            P("section", "pack", "tensor"),
            P("section", "pack", "tensor"),
            P(),
        ),
        out_specs=P("section", ("pack", "tensor"), None),
        check_vma=False,
    )
```

profile of v0, /device:TPU:24, one launch (start us, length us, event | category | flops | bytes accessed | tf_op | source)
XLA Modules:
  0.0 758.1 jit_solution(745449855824786794)
XLA Ops:
  2.9 1.6 copy.91
  4.6 2.0 copy.92
  6.6 1.6 copy.96
  8.2 3.0 copy.97
  11.2 16.2 %gather_fusion.1 = bf16[2048,10,128]{2,1,0:T(8,128)(2,1)} fusion(bf16[512,10,128]{2,1,0:T(8,128)(2,1)S(1)} %copy.92, s32[2048]{0:T(1024)S(1)} %fusion.49), kind=kCustom, calls=%fused_computation.clone | custom fusion | bytes 10493952 | tf_op jit(solution)/shard_map/jit(_take)/gather | solution.py:104
  27.4 18.0 %gather_fusion.2 = bf16[2048,10,128]{2,1,0:T(8,128)(2,1)} fusion(bf16[512,10,128]{2,1,0:T(8,128)(2,1)} %copy.97, s32[2048]{0:T(1024)S(1)} %fusion.49), kind=kCustom, calls=%fused_computation.1.clone | custom fusion | bytes 10493952 | tf_op jit(solution)/shard_map/jit(_take)/gather | solution.py:102
  46.0 2.0 copy.102
  48.0 16.2 %gather_fusion.3 = bf16[2048,10,128]{2,1,0:T(8,128)(2,1)} fusion(bf16[512,10,128]{2,1,0:T(8,128)(2,1)S(1)} %copy.102, s32[2048]{0:T(1024)S(1)} %fusion.49), kind=kCustom, calls=%fused_computation.2.clone | custom fusion | bytes 10493952 | tf_op jit(solution)/shard_map/jit(_take)/gather | solution.py:103
  64.2 16.9 %broadcast_select_fusion = (bf16[2048,10,128]{2,1,0:T(8,128)(2,1)S(1)}, bf16[2048,10,128]{2,1,0:T(8,128)(2,1)}, bf16[2048,10,128]{2,1,0:T(8,128)(2,1)}) fusion(bf16[2048,10,128]{2,1,0:T(8,128)(2,1)} %gather_fusion.3, pred[2048]{0:T(1024)(128)(4,1)S(1)} %compare_and_fusion, bf16[2048,10,128]{2,1,0:T(8,128)(2,1)} %gather_fusion.2, ...), kind=kLoop, calls=%fused_computation.32 | loop fusion | flops 7864320 | bytes 31459328 | tf_op jit(solution)/shard_map/jit(_take)/select_n | solution.py:103
  81.1 3.7 copy.104
  84.8 11.5 %all-to-all-start.2 = ((bf16[32,64,10,128]{3,1,2,0:T(8,128)(2,1)}), bf16[32,64,10,128]{3,1,2,0:T(8,128)(2,1)}, u32[]{:S(2)}, u32[]{:S(2)}) async-start(bf16[32,64,10,128]{3,1,2,0:T(8,128)(2,1)} %copy.104), calls=%async_computation.2 | async-start | bytes 10485760 | tf_op jit(solution)/shard_map/all_to_all | solution.py:122
  96.4 7.1 copy.94
  103.5 111.7 %all-to-all-done.2 = bf16[32,64,10,128]{3,1,2,0:T(8,128)(2,1)} async-done(((bf16[32,64,10,128]{3,1,2,0:T(8,128)(2,1)}), bf16[32,64,10,128]{3,1,2,0:T(8,128)(2,1)}, u32[]{:S(2)}, u32[]{:S(2)}) %all-to-all-start.2) | async-done | bytes 5242912 | tf_op jit(solution)/shard_map/all_to_all | solution.py:122
  215.2 8.2 %all-to-all-start = ((bf16[32,64,10,128]{3,1,2,0:T(8,128)(2,1)}), bf16[32,64,10,128]{3,1,2,0:T(8,128)(2,1)}, u32[]{:S(2)}, u32[]{:S(2)}) async-start(bf16[32,64,10,128]{3,1,2,0:T(8,128)(2,1)} %copy.94), calls=%async_computation | async-start | bytes 10485760 | tf_op jit(solution)/shard_map/all_to_all | solution.py:123
  223.4 7.1 copy.99
  230.4 111.0 %all-to-all-done = bf16[32,64,10,128]{3,1,2,0:T(8,128)(2,1)} async-done(((bf16[32,64,10,128]{3,1,2,0:T(8,128)(2,1)}), bf16[32,64,10,128]{3,1,2,0:T(8,128)(2,1)}, u32[]{:S(2)}, u32[]{:S(2)}) %all-to-all-start) | async-done | bytes 5242912 | tf_op jit(solution)/shard_map/all_to_all | solution.py:123
  341.5 8.3 %all-to-all-start.1 = ((bf16[32,64,10,128]{3,1,2,0:T(8,128)(2,1)}), bf16[32,64,10,128]{3,1,2,0:T(8,128)(2,1)}, u32[]{:S(2)}, u32[]{:S(2)}) async-start(bf16[32,64,10,128]{3,1,2,0:T(8,128)(2,1)} %copy.99), calls=%async_computation.1 | async-start | bytes 10485760 | tf_op jit(solution)/shard_map/all_to_all | solution.py:121
  351.0 1.3 broadcast_select_fusion.4
  352.4 13.1 %scatter.4 = s32[32,16]{0,1:T(8,128)S(1)} dynamic-update-slice(s32[32,16]{0,1:T(8,128)S(1)} %multiply_add_fusion, s32[32,1]{0,1:T(1,128)S(1)} %broadcast_select_fusion.4, s32[]{:T(128)} %constant.144.clone.1, s32[]{:T(128)} %constant.144.clone.1) | dynamic-update-slice | bytes 260 | tf_op jit(solution)/shard_map/scatter | solution.py:23
  366.5 4.2 copy.105
  370.7 4.2 copy.95
  375.0 6.0 pad_maximum_fusion
  381.0 86.8 %all-to-all-done.1 = bf16[32,64,10,128]{3,1,2,0:T(8,128)(2,1)} async-done(((bf16[32,64,10,128]{3,1,2,0:T(8,128)(2,1)}), bf16[32,64,10,128]{3,1,2,0:T(8,128)(2,1)}, u32[]{:S(2)}, u32[]{:S(2)}) %all-to-all-start.1) | async-done | bytes 5242912 | tf_op jit(solution)/shard_map/all_to_all | solution.py:121
  467.8 6.5 copy.100
  474.3 91.4 %while.11 = (s32[]{:T(128)}, bf16[4,512,10,128]{3,1,0,2:T(8,128)(2,1)}, s32[4]{0:T(128)S(1)}, bf16[2176,10,128]{2,0,1:T(8,128)(2,1)}, s32[2048]{0:T(1024)S(1)}, ...) while((s32[]{:T(128)}, ...), condition=%wide.region_13.15_spmd, body=%wide.region_10.14_spmd.sunk | while | flops 2547063040 | bytes 15130336 | solution.py:63
  476.1 6.4 fusion.68
  482.5 12.5 %fusion.69 = bf16[1,512,10,128]{1,3,2,0:T(8,128)(2,1)S(1)} fusion(f32[10,512]{1,0:T(8,128)S(1)} %fusion.68, bf16[2176,10,128]{2,0,1:T(8,128)(2,1)} %get-tuple-element.212, s32[]{:T(128)S(6)} %select_n.219, pred[512,640]{1,0:T(8,128)(4,1)S(1)} %broadcast_compare_fusion.3, bf16[2176,10,128]{2,0,1:T(8,128)(2,1)} %get-tuple-element.216, ...), kind=kOutput, calls=%fused_computation.19.clone.1 | convolution fusion | flops 1694766720 | bytes 6247936 | tf_op jit(solution)/shard_map/while/body/eval_jaxpr/hqk,khd->qhd/dot_general | solution.py:60
  495.9 1.3 constant_dynamic-update-slice_fusion.2
  498.9 6.4 fusion.68
  505.3 12.5 %fusion.69 = bf16[1,512,10,128]{1,3,2,0:T(8,128)(2,1)S(1)} fusion(f32[10,512]{1,0:T(8,128)S(1)} %fusion.68, bf16[2176,10,128]{2,0,1:T(8,128)(2,1)} %get-tuple-element.212, s32[]{:T(128)S(6)} %select_n.219, pred[512,640]{1,0:T(8,128)(4,1)S(1)} %broadcast_compare_fusion.3, bf16[2176,10,128]{2,0,1:T(8,128)(2,1)} %get-tuple-element.216, ...), kind=kOutput, calls=%fused_computation.19.clone.1 | convolution fusion | flops 1694766720 | bytes 6247936 | tf_op jit(solution)/shard_map/while/body/eval_jaxpr/hqk,khd->qhd/dot_general | solution.py:60
  518.7 1.3 constant_dynamic-update-slice_fusion.2
  521.7 6.4 fusion.68
  528.2 12.5 %fusion.69 = bf16[1,512,10,128]{1,3,2,0:T(8,128)(2,1)S(1)} fusion(f32[10,512]{1,0:T(8,128)S(1)} %fusion.68, bf16[2176,10,128]{2,0,1:T(8,128)(2,1)} %get-tuple-element.212, s32[]{:T(128)S(6)} %select_n.219, pred[512,640]{1,0:T(8,128)(4,1)S(1)} %broadcast_compare_fusion.3, bf16[2176,10,128]{2,0,1:T(8,128)(2,1)} %get-tuple-element.216, ...), kind=kOutput, calls=%fused_computation.19.clone.1 | convolution fusion | flops 1694766720 | bytes 6247936 | tf_op jit(solution)/shard_map/while/body/eval_jaxpr/hqk,khd->qhd/dot_general | solution.py:60
  541.5 1.3 constant_dynamic-update-slice_fusion.2
  544.6 6.4 fusion.68
  551.0 12.5 %fusion.69 = bf16[1,512,10,128]{1,3,2,0:T(8,128)(2,1)S(1)} fusion(f32[10,512]{1,0:T(8,128)S(1)} %fusion.68, bf16[2176,10,128]{2,0,1:T(8,128)(2,1)} %get-tuple-element.212, s32[]{:T(128)S(6)} %select_n.219, pred[512,640]{1,0:T(8,128)(4,1)S(1)} %broadcast_compare_fusion.3, bf16[2176,10,128]{2,0,1:T(8,128)(2,1)} %get-tuple-element.216, ...), kind=kOutput, calls=%fused_computation.19.clone.1 | convolution fusion | flops 1694766720 | bytes 6247936 | tf_op jit(solution)/shard_map/while/body/eval_jaxpr/hqk,khd->qhd/dot_general | solution.py:60
  564.4 1.3 constant_dynamic-update-slice_fusion.2
  565.7 6.6 copy.108
  572.3 6.6 all-to-all-start.3
  579.2 117.4 %all-to-all-done.3 = bf16[32,64,10,128]{3,1,2,0:T(8,128)(2,1)} async-done(((bf16[32,64,10,128]{3,1,2,0:T(8,128)(2,1)}), bf16[32,64,10,128]{3,1,2,0:T(8,128)(2,1)}, u32[]{:S(2)}, u32[]{:S(2)}) %all-to-all-start.3) | async-done | bytes 5242912 | tf_op jit(solution)/shard_map/all_to_all | solution.py:133
  696.6 14.9 %copy.109 = bf16[32,64,10,128]{3,2,1,0:T(8,128)(2,1)} copy(bf16[32,64,10,128]{3,1,2,0:T(8,128)(2,1)} %all-to-all-done.3) | data formatting | bytes 10485760 | tf_op jit(solution)/shard_map/all_to_all | solution.py:133
  711.5 4.6 gather_fusion
  716.9 1.1 copy.119
  718.0 1.2 broadcast_select_fusion.3
  719.3 4.8 all_to_all.36
  724.1 1.5 collective-permute-start
  725.6 30.5 %collective-permute-done = bf16[256,2560]{0,1:T(8,128)(2,1)S(1)} collective-permute-done((bf16[256,2560]{0,1:T(8,128)(2,1)S(1)}, bf16[256,2560]{0,1:T(8,128)(2,1)S(1)}, u32[]{:S(2)}, u32[]{:S(2)}) %collective-permute-start) | collective-permute-done | bytes 1310752 | tf_op jit(solution)/shard_map/ppermute | solution.py:17
  756.1 1.6 copy.112
  (75 shorter events, 14.4 us)
Async XLA Ops:
  1.8 0.6 copy-start.5
  1.8 0.6 copy-start.3
  2.2 0.5 copy-start.1
  27.4 18.0 %copy-start = (bf16[1,512,1280]{2,1,0:T(8,128)(2,1)S(1)}, bf16[1,512,1280]{2,1,0:T(8,128)(2,1)}, u32[]{:S(2)}) copy-start(bf16[1,512,1280]{2,1,0:T(8,128)(2,1)} %param.11) | copy-start | bytes 3932164
  84.8 130.3 %all-to-all-start.2 = ((bf16[32,64,10,128]{3,1,2,0:T(8,128)(2,1)}), bf16[32,64,10,128]{3,1,2,0:T(8,128)(2,1)}, u32[]{:S(2)}, u32[]{:S(2)}) async-start(bf16[32,64,10,128]{3,1,2,0:T(8,128)(2,1)} %copy.104), calls=%async_computation.2 | async-start | bytes 10485760 | tf_op jit(solution)/shard_map/all_to_all | solution.py:122
  215.2 126.3 %all-to-all-start = ((bf16[32,64,10,128]{3,1,2,0:T(8,128)(2,1)}), bf16[32,64,10,128]{3,1,2,0:T(8,128)(2,1)}, u32[]{:S(2)}, u32[]{:S(2)}) async-start(bf16[32,64,10,128]{3,1,2,0:T(8,128)(2,1)} %copy.94), calls=%async_computation | async-start | bytes 10485760 | tf_op jit(solution)/shard_map/all_to_all | solution.py:123
  341.5 126.3 %all-to-all-start.1 = ((bf16[32,64,10,128]{3,1,2,0:T(8,128)(2,1)}), bf16[32,64,10,128]{3,1,2,0:T(8,128)(2,1)}, u32[]{:S(2)}, u32[]{:S(2)}) async-start(bf16[32,64,10,128]{3,1,2,0:T(8,128)(2,1)} %copy.99), calls=%async_computation.1 | async-start | bytes 10485760 | tf_op jit(solution)/shard_map/all_to_all | solution.py:121
  572.3 6.6 copy-start.6
  572.3 6.7 copy-start.2
  572.3 6.7 copy-start.4
  572.3 124.3 %all-to-all-start.3 = ((bf16[32,64,10,128]{3,1,2,0:T(8,128)(2,1)}), bf16[32,64,10,128]{3,1,2,0:T(8,128)(2,1)}, u32[]{:S(2)}, u32[]{:S(2)}) async-start(bf16[32,64,10,128]{3,1,2,0:T(8,128)(2,1)} %copy.108), calls=%async_computation.3 | async-start | bytes 10485760 | tf_op jit(solution)/shard_map/all_to_all | solution.py:133
  724.1 32.0 %collective-permute-start = (bf16[256,2560]{0,1:T(8,128)(2,1)S(1)}, bf16[256,2560]{0,1:T(8,128)(2,1)S(1)}, u32[]{:S(2)}, u32[]{:S(2)}) collective-permute-start(bf16[256,2560]{0,1:T(8,128)(2,1)S(1)} %bitcast.52), channel_id=1, source_target_pairs={{0,64},{64,128},{128,192},{192,0},{1,65},{65,129},{129,193},{193,1... | collective-permute-start | bytes 3932168 | tf_op jit(solution)/shard_map/ppermute | solution.py:17
where the time goes:
time: 767 us; the launch traced here: 758 us
  waiting for transfers between devices  457 us (60%)
  local copies, waits for them, and re-layouts  151 us (20%)
  matrix products  75.9 us (10%)
  starting transfers between devices  36.1 us (5%)
  other arithmetic  29.6 us (4%)
    all_to_all x1, waiting for transfers between devices, per_device(): lax.all_to_all(mixed.reshape(slot_shape), 'pack', split_axis=0, concat_ax...  117 us
    all_to_all x1, waiting for transfers between devices, per_device(): lax.all_to_all(send_key, 'pack', split_axis=0, concat_axis=0, tiled=True)  112 us
    all_to_all x1, waiting for transfers between devices, per_device(): lax.all_to_all(send_value, 'pack', split_axis=0, concat_axis=0, tiled=True)  111 us
    all_to_all x1, waiting for transfers between devices, per_device(): lax.all_to_all(send_query, 'pack', split_axis=0, concat_axis=0, tiled=True)  86.8 us
    dot_general x4, matrix products, one_block(): jnp.einsum('hqk,khd->qhd', weights, value_block, preferred_element_type=j...  50.2 us
    ppermute x1, waiting for transfers between devices, passed_along(): return lax.ppermute(value, axis, pairs)  30.5 us
    sub x4, matrix products, one_block(): weights = jnp.exp(scores - row_max)  25.7 us
    gather x1, local copies, waits for them, and re-layouts, per_device(): send_query = jnp.take(query_three, picked, axis=0).reshape(slot_shape)  18 us
  transfers between devices with their start and end apart: 5, of which 5 were waited for; matrix products, arithmetic and copies ran while one was open for 6% of the time, Pallas kernels for 0%

commit v1 on v0

v1 whole, which is shorter than its diff:
```python
import functools
import math

import jax
import jax.numpy as jnp
from jax import lax
from jax.experimental import pallas as pl
from jax.experimental.pallas import tpu as pltpu
from jax.sharding import PartitionSpec as P

HEAD_DIM = 128
HALO = 64
BLOCK = 128
WINDOW = BLOCK + 2 * HALO
MESH = pl.DeviceIdType.MESH
MASKED = -3.0e38


def kernel(
    sizes,
    len_ref,
    q_hbm,
    k_hbm,
    v_hbm,
    out_ref,
    q_buf,
    k_buf,
    v_buf,
    bias,
    stage,
    relay_one,
    relay_two,
    load_sem,
    halo_send,
    halo_recv,
    out_send,
    out_recv,
    one_recv,
    one_send,
    two_recv,
    two_send,
):
    sections, homes, heads, rows, segs = sizes
    feats = heads * HEAD_DIM
    s, p, t = lax.axis_index("section"), lax.axis_index("pack"), lax.axis_index("tensor")
    ahead, behind = lax.rem(s + 1, sections), lax.rem(s + sections - 1, sections)
    after, before = lax.rem(p + 1, homes), lax.rem(p + homes - 1, homes)

    barrier = pltpu.get_barrier_semaphore()
    partners = [
        (ahead, p, t),
        (ahead, p, 1 - t),
        (behind, p, t),
        (behind, p, 1 - t),
        (s, after, t),
        (s, before, t),
    ]
    for partner in partners:
        pl.semaphore_signal(barrier, inc=1, device_id=partner, device_id_type=MESH)

    own = pl.ds(HALO, rows)
    loads = [
        pltpu.make_async_copy(q_hbm.at[0], q_buf, load_sem.at[0]),
        pltpu.make_async_copy(k_hbm.at[0], k_buf.at[own], load_sem.at[1]),
        pltpu.make_async_copy(v_hbm.at[0], v_buf.at[own], load_sem.at[2]),
    ]
    for load in loads:
        load.start()

    thresholds = [jnp.where(p > 0, -len_ref[s, segs - 1, before], 0)]
    end = jnp.int32(0)
    for j in range(segs - 1):
        end = end + len_ref[s, j, p]
        thresholds.append(end)
    thresholds.append(rows + jnp.where(p < homes - 1, len_ref[s, 0, after], 0))

    def labels(position):
        total = jnp.zeros(position.shape, jnp.int32)
        for threshold in thresholds:
            total = total + jnp.where(position >= threshold, 1, 0)
        return total

    key_label = labels(lax.broadcasted_iota(jnp.int32, (8, rows + 2 * HALO), 1) - HALO)
    for b in range(rows // BLOCK):
        query_label = labels(lax.broadcasted_iota(jnp.int32, (BLOCK, 128), 0) + b * BLOCK)
        for c in range(WINDOW // 128):
            start = b * BLOCK + c * 128
            same = query_label == key_label[0:1, start : start + 128]
            bias[b, :, c * 128 : c * 128 + 128] = jnp.where(same, 0.0, MASKED)

    pl.semaphore_wait(barrier, len(partners))

    def head_cols(h):
        return pl.ds(pl.multiple_of(h * HEAD_DIM, HEAD_DIM), HEAD_DIM)

    def halo_copies(h):
        cols = head_cols(h)
        copies = []
        for n, (source, buf) in enumerate(((k_hbm, k_buf), (v_hbm, v_buf))):
            copies.append(
                pltpu.make_async_remote_copy(
                    src_ref=source.at[0, pl.ds(rows - HALO, HALO), cols],
                    dst_ref=buf.at[pl.ds(0, HALO), cols],
                    send_sem=halo_send.at[n, h],
                    recv_sem=halo_recv.at[n, h],
                    device_id=(s, after, t),
                    device_id_type=MESH,
                )
            )
            copies.append(
                pltpu.make_async_remote_copy(
                    src_ref=source.at[0, pl.ds(0, HALO), cols],
                    dst_ref=buf.at[pl.ds(HALO + rows, HALO), cols],
                    send_sem=halo_send.at[n + 2, h],
                    recv_sem=halo_recv.at[n + 2, h],
                    device_id=(s, before, t),
                    device_id_type=MESH,
                )
            )
        return copies

    def start_halo(h, carry):
        for copy in halo_copies(h):
            copy.start()
        return carry

    lax.fori_loop(0, heads, start_halo, 0)

    for load in loads:
        load.wait()

    factor = math.log2(math.e) / math.sqrt(HEAD_DIM)

    def attend(b, h):
        cols = head_cols(h)
        scores = lax.dot_general(
            q_buf[b * BLOCK : (b + 1) * BLOCK, cols],
            k_buf[b * BLOCK : b * BLOCK + WINDOW, cols],
            (((1,), (1,)), ((), ())),
            preferred_element_type=jnp.float32,
        )
        scores = scores + bias[b]
        row_max = jnp.max(scores, axis=1, keepdims=True)
        weights = jnp.exp2((scores - row_max) * factor)
        weights = weights * (1.0 / jnp.sum(weights, axis=1, keepdims=True))
        mixed = jnp.dot(
            weights.astype(jnp.bfloat16),
            v_buf[b * BLOCK : b * BLOCK + WINDOW, cols],
            preferred_element_type=jnp.float32,
        )
        stage[b, h] = mixed.astype(jnp.bfloat16)

    def final_place(b, h):
        start = pl.multiple_of(t * feats + h * HEAD_DIM, HEAD_DIM)
        return out_ref.at[pl.ds((b % 2) * BLOCK, BLOCK), pl.ds(start, HEAD_DIM)]

    def forward(b, h):
        return pltpu.make_async_remote_copy(
            src_ref=stage.at[b, h],
            dst_ref=final_place(b, h),
            send_sem=out_send,
            recv_sem=out_recv,
            device_id=(ahead, p, b // 2),
            device_id_type=MESH,
        )

    def hop_one(h):
        return pltpu.make_async_remote_copy(
            src_ref=stage.at[1, h],
            dst_ref=relay_one.at[h],
            send_sem=out_send,
            recv_sem=one_recv.at[h],
            device_id=(behind, p, t),
            device_id_type=MESH,
        )

    def hop_two(h):
        return pltpu.make_async_remote_copy(
            src_ref=relay_one.at[h],
            dst_ref=relay_two.at[h],
            send_sem=one_send,
            recv_sem=two_recv.at[h],
            device_id=(behind, p, t),
            device_id_type=MESH,
        )

    def hop_three(h):
        return pltpu.make_async_remote_copy(
            src_ref=relay_two.at[h],
            dst_ref=final_place(1, h),
            send_sem=two_send,
            recv_sem=out_recv,
            device_id=(behind, p, 0),
            device_id_type=MESH,
        )

    def inner(h, carry):
        attend(1, h)
        attend(2, h)
        hop_one(h).start()
        forward(2, h).start()
        return carry

    lax.fori_loop(0, heads, inner, 0)

    def outer(h, carry):
        for copy in halo_copies(h):
            copy.wait_recv()
        attend(0, h)
        attend(3, h)
        forward(0, h).start()
        forward(3, h).start()
        hop_one(h).wait_recv()
        hop_two(h).start()
        return carry

    lax.fori_loop(0, heads, outer, 0)

    def last(h, carry):
        hop_two(h).wait_recv()
        hop_three(h).start()
        for copy in halo_copies(h):
            copy.wait_send()
        return carry

    lax.fori_loop(0, heads, last, 0)

    def whole(ref, send, recv):
        return pltpu.make_async_remote_copy(
            src_ref=ref,
            dst_ref=ref,
            send_sem=send,
            recv_sem=recv,
            device_id=(ahead, p, t),
            device_id_type=MESH,
        )

    whole(stage, out_send, out_recv).wait_send()
    whole(relay_one, one_send, out_recv).wait_send()
    whole(relay_two, two_send, out_recv).wait_send()
    whole(out_ref, out_send, out_recv).wait_recv()


def per_device(sections, homes, queries, keys, values, seg_len):
    _, rows, feats = queries.shape
    heads = feats // HEAD_DIM
    segs = seg_len.shape[2]
    blocks = rows // BLOCK
    bf16 = jnp.bfloat16
    dma = pltpu.SemaphoreType.DMA
    handed = pl.pallas_call(
        functools.partial(kernel, (sections, homes, heads, rows, segs)),
        out_shape=jax.ShapeDtypeStruct((rows // 2, 2 * feats), bf16),
        in_specs=[pl.BlockSpec(memory_space=pltpu.SMEM)] + [pl.BlockSpec(memory_space=pl.ANY)] * 3,
        out_specs=pl.BlockSpec(memory_space=pl.ANY),
        scratch_shapes=[
            pltpu.VMEM((rows, feats), bf16),
            pltpu.VMEM((rows + 2 * HALO, feats), bf16),
            pltpu.VMEM((rows + 2 * HALO, feats), bf16),
            pltpu.VMEM((blocks, BLOCK, WINDOW), jnp.float32),
            pltpu.VMEM((blocks, heads, BLOCK, HEAD_DIM), bf16),
            pltpu.VMEM((heads, BLOCK, HEAD_DIM), bf16),
            pltpu.VMEM((heads, BLOCK, HEAD_DIM), bf16),
            dma((3,)),
            dma((4, heads)),
            dma((4, heads)),
            dma,
            dma,
            dma((heads,)),
            dma,
            dma((heads,)),
            dma,
        ],
        compiler_params=pltpu.CompilerParams(
            collective_id=0, has_side_effects=True, vmem_limit_bytes=56 * 1024 * 1024
        ),
        cost_estimate=pl.CostEstimate(
            flops=4 * rows * WINDOW * feats,
            bytes_accessed=8 * rows * feats,
            transcendentals=rows * WINDOW * heads,
        ),
        name="segment_attention",
    )(jnp.swapaxes(seg_len, 1, 2), queries, keys, values)
    return handed[None]


def solution(mesh):
    sections, homes = mesh.shape["section"], mesh.shape["pack"]
    return jax.shard_map(
        functools.partial(per_device, sections, homes),
        mesh=mesh,
        in_specs=(
            P("section", "pack", "tensor"),
            P("section", "pack", "tensor"),
            P("section", "pack", "tensor"),
            P(),
        ),
        out_specs=P("section", ("pack", "tensor"), None),
        check_vma=False,
    )
```

time: 767 us -> 40.6 us (0.05)
  the two profiles are of different devices: /device:TPU:24 before, /device:TPU:1 now
where the time goes in v1:
time: 40.6 us; the launch traced here: 40.4 us
  Pallas kernels  37.9 us (93%)
  local copies, waits for them, and re-layouts  2.46 us (6%)
    pallas_call x1, Pallas kernels, per_device(): pl.pallas_call(functools.partial(kernel, (sections, homes, heads, rows, s...  37.9 us
    unnamed x1, local copies, waits for them, and re-layouts  2.46 us

profile of v1, /device:TPU:1, one launch (start us, length us, event | category | flops | bytes accessed | tf_op | source)
XLA Modules:
  0.0 40.4 jit_solution(17989664981382461822)
XLA Ops:
  0.0 37.9 %segment_attention.1 = bf16[256,2560]{1,0:T(8,128)(2,1)} custom-call(s32[4,16,32]{2,1,0:T(8,128)} %bitcast.3, bf16[1,512,1280]{2,1,0:T(8,128)(2,1)} %q_hbm.1, bf16[1,512,1280]{2,1,0:T(8,128)(2,1)} %k_hbm.1, bf16[1,512,1280]{2,1,0:T(8,128)(2,1)} %v_hbm.1), custom_call_target="tpu_custom_call" | custom-call | flops 671088640 | bytes 5242880 | tf_op jit(solution)/shard_map/segment_attention/pallas_call | solution.py:251
  37.9 2.5 %copy.6 = bf16[1,256,2560]{2,1,0:T(8,128)(2,1)} copy(bf16[1,256,2560]{2,1,0:T(8,128)(2,1)} %bitcast.2) | data formatting | bytes 2621440

commit v2 on v1

v2 whole, which is shorter than its diff:
```python
import functools
import math

import jax
import jax.numpy as jnp
from jax import lax
from jax.experimental import pallas as pl
from jax.experimental.pallas import tpu as pltpu
from jax.sharding import PartitionSpec as P

HEAD_DIM = 128
HALO = 64
BLOCK = 128
WINDOW = BLOCK + 2 * HALO
MESH = pl.DeviceIdType.MESH
MASKED = -3.0e38
GROUP = 2


def kernel(
    sizes,
    len_hbm,
    q_hbm,
    k_hbm,
    v_hbm,
    out_ref,
    q_buf,
    k_buf,
    v_buf,
    bias,
    stage,
    relay_one,
    relay_two,
    len_ref,
    len_sem,
    load_sem,
    halo_send,
    halo_recv,
    out_send,
    out_recv,
    one_recv,
    one_send,
    two_recv,
    two_send,
):
    sections, homes, heads, rows, segs = sizes
    feats = heads * HEAD_DIM
    s, p, t = lax.axis_index("section"), lax.axis_index("pack"), lax.axis_index("tensor")
    ahead, behind = lax.rem(s + 1, sections), lax.rem(s + sections - 1, sections)
    after, before = lax.rem(p + 1, homes), lax.rem(p + homes - 1, homes)

    barrier = pltpu.get_barrier_semaphore()
    has_after, has_before = p < homes - 1, p > 0

    def greet(partner):
        pl.semaphore_signal(barrier, inc=1, device_id=partner, device_id_type=MESH)

    partners = [(ahead, p, t), (ahead, p, 1 - t), (behind, p, t), (behind, p, 1 - t)]
    for partner in partners:
        greet(partner)

    @pl.when(has_after)
    def _():
        greet((s, after, t))

    @pl.when(has_before)
    def _():
        greet((s, before, t))

    fetch_lengths = pltpu.make_async_copy(len_hbm.at[s], len_ref, len_sem)
    fetch_lengths.start()

    units = heads // GROUP
    width = GROUP * HEAD_DIM

    def unit_cols(u):
        return pl.ds(pl.multiple_of(u * width, width), width)

    def loads(u):
        cols, own = unit_cols(u), pl.ds(HALO, rows)
        return [
            pltpu.make_async_copy(q_hbm.at[0, :, cols], q_buf.at[:, cols], load_sem.at[0, u]),
            pltpu.make_async_copy(k_hbm.at[0, :, cols], k_buf.at[own, cols], load_sem.at[1, u]),
            pltpu.make_async_copy(v_hbm.at[0, :, cols], v_buf.at[own, cols], load_sem.at[2, u]),
        ]

    def start_loads(u, carry):
        for load in loads(u):
            load.start()
        return carry

    lax.fori_loop(0, units, start_loads, 0)

    @pl.when(jnp.logical_not(has_before))
    def _():
        k_buf[0:HALO] = jnp.zeros((HALO, feats), jnp.bfloat16)
        v_buf[0:HALO] = jnp.zeros((HALO, feats), jnp.bfloat16)

    @pl.when(jnp.logical_not(has_after))
    def _():
        k_buf[HALO + rows :] = jnp.zeros((HALO, feats), jnp.bfloat16)
        v_buf[HALO + rows :] = jnp.zeros((HALO, feats), jnp.bfloat16)

    fetch_lengths.wait()

    thresholds = [jnp.where(has_before, -len_ref[segs - 1, before], 0)]
    end = jnp.int32(0)
    for j in range(segs - 1):
        end = end + len_ref[j, p]
        thresholds.append(end)
    thresholds.append(rows + jnp.where(has_after, len_ref[0, after], 0))

    def labels(position):
        total = jnp.zeros(position.shape, jnp.int32)
        for threshold in thresholds:
            total = total + jnp.where(position >= threshold, 1, 0)
        return total

    key_label = labels(lax.broadcasted_iota(jnp.int32, (8, rows + 2 * HALO), 1) - HALO)
    for b in range(rows // BLOCK):
        query_label = labels(lax.broadcasted_iota(jnp.int32, (BLOCK, 128), 0) + b * BLOCK)
        for c in range(WINDOW // 128):
            start = b * BLOCK + c * 128
            same = query_label == key_label[0:1, start : start + 128]
            bias[b, :, c * 128 : c * 128 + 128] = jnp.where(same, 0.0, MASKED)

    def halo(u, side):
        cols = unit_cols(u)
        low, high = pl.ds(0, HALO), pl.ds(rows - HALO, HALO)
        source_rows, target_rows, home = (
            (high, pl.ds(0, HALO), after) if side == 0 else (low, pl.ds(HALO + rows, HALO), before)
        )
        return [
            pltpu.make_async_remote_copy(
                src_ref=source.at[0, source_rows, cols],
                dst_ref=buf.at[target_rows, cols],
                send_sem=halo_send.at[2 * side + n, u],
                recv_sem=halo_recv.at[2 * side + n, u],
                device_id=(s, home, t),
                device_id_type=MESH,
            )
            for n, (source, buf) in enumerate(((k_hbm, k_buf), (v_hbm, v_buf)))
        ]

    def each_side(act, conditions):
        for side, condition in enumerate(conditions):

            @pl.when(condition)
            def _():
                act(side)

    factor = math.log2(math.e) / math.sqrt(HEAD_DIM)

    def attend(b, u):
        for g in range(GROUP):
            cols = pl.ds(pl.multiple_of(u * width, width) + g * HEAD_DIM, HEAD_DIM)
            scores = lax.dot_general(
                q_buf[b * BLOCK : (b + 1) * BLOCK, cols],
                k_buf[b * BLOCK : b * BLOCK + WINDOW, cols],
                (((1,), (1,)), ((), ())),
                preferred_element_type=jnp.float32,
            )
            scores = scores + bias[b]
            row_max = jnp.max(scores, axis=1, keepdims=True)
            weights = jnp.exp2((scores - row_max) * factor)
            weights = weights * (1.0 / jnp.sum(weights, axis=1, keepdims=True))
            mixed = jnp.dot(
                weights.astype(jnp.bfloat16),
                v_buf[b * BLOCK : b * BLOCK + WINDOW, cols],
                preferred_element_type=jnp.float32,
            )
            stage[b, u, :, g * HEAD_DIM : (g + 1) * HEAD_DIM] = mixed.astype(jnp.bfloat16)

    def final_place(b, u):
        start = pl.multiple_of(t * feats + u * width, HEAD_DIM)
        return out_ref.at[pl.ds((b % 2) * BLOCK, BLOCK), pl.ds(start, width)]

    def forward(b, u):
        return pltpu.make_async_remote_copy(
            src_ref=stage.at[b, u],
            dst_ref=final_place(b, u),
            send_sem=out_send,
            recv_sem=out_recv,
            device_id=(ahead, p, b // 2),
            device_id_type=MESH,
        )

    def hop_one(u):
        return pltpu.make_async_remote_copy(
            src_ref=stage.at[1, u],
            dst_ref=relay_one.at[u],
            send_sem=out_send,
            recv_sem=one_recv.at[u],
            device_id=(behind, p, t),
            device_id_type=MESH,
        )

    def hop_two(u):
        return pltpu.make_async_remote_copy(
            src_ref=relay_one.at[u],
            dst_ref=relay_two.at[u],
            send_sem=one_send,
            recv_sem=two_recv.at[u],
            device_id=(behind, p, t),
            device_id_type=MESH,
        )

    def hop_three(u):
        return pltpu.make_async_remote_copy(
            src_ref=relay_two.at[u],
            dst_ref=final_place(1, u),
            send_sem=two_send,
            recv_sem=out_recv,
            device_id=(behind, p, 0),
            device_id_type=MESH,
        )

    def make_inner(u):
        for load in loads(u):
            load.wait()
        attend(1, u)
        attend(2, u)

    def send_inner(u):
        hop_one(u).start()
        forward(2, u).start()
        each_side(lambda side: [copy.start() for copy in halo(u, side)], (has_after, has_before))

    make_inner(0)

    pack_peers = jnp.where(has_after, 1, 0) + jnp.where(has_before, 1, 0)
    pl.semaphore_wait(barrier, len(partners) + pack_peers)

    def inner(u, carry):
        send_inner(u - 1)
        make_inner(u)
        return carry

    lax.fori_loop(1, units, inner, 0)
    send_inner(units - 1)

    def outer(u, carry):
        each_side(lambda side: [copy.wait_recv() for copy in halo(u, side)], (has_before, has_after))
        attend(0, u)
        attend(3, u)
        forward(0, u).start()
        forward(3, u).start()
        hop_one(u).wait_recv()
        hop_two(u).start()
        return carry

    lax.fori_loop(0, units, outer, 0)

    def last(u, carry):
        hop_two(u).wait_recv()
        hop_three(u).start()
        each_side(lambda side: [copy.wait_send() for copy in halo(u, side)], (has_after, has_before))
        return carry

    lax.fori_loop(0, units, last, 0)

    def whole(ref, send, recv):
        return pltpu.make_async_remote_copy(
            src_ref=ref,
            dst_ref=ref,
            send_sem=send,
            recv_sem=recv,
            device_id=(ahead, p, t),
            device_id_type=MESH,
        )

    whole(stage, out_send, out_recv).wait_send()
    whole(relay_one, one_send, out_recv).wait_send()
    whole(relay_two, two_send, out_recv).wait_send()
    whole(out_ref, out_send, out_recv).wait_recv()


def per_device(sections, homes, queries, keys, values, seg_len):
    _, rows, feats = queries.shape
    heads = feats // HEAD_DIM
    segs = seg_len.shape[2]
    blocks, units, width = rows // BLOCK, heads // GROUP, GROUP * HEAD_DIM
    bf16 = jnp.bfloat16
    dma = pltpu.SemaphoreType.DMA
    handed = pl.pallas_call(
        functools.partial(kernel, (sections, homes, heads, rows, segs)),
        out_shape=jax.ShapeDtypeStruct((rows // 2, 2 * feats), bf16),
        in_specs=[pl.BlockSpec(memory_space=pl.ANY)] * 4,
        out_specs=pl.BlockSpec(memory_space=pl.ANY),
        scratch_shapes=[
            pltpu.VMEM((rows, feats), bf16),
            pltpu.VMEM((rows + 2 * HALO, feats), bf16),
            pltpu.VMEM((rows + 2 * HALO, feats), bf16),
            pltpu.VMEM((blocks, BLOCK, WINDOW), jnp.float32),
            pltpu.VMEM((blocks, units, BLOCK, width), bf16),
            pltpu.VMEM((units, BLOCK, width), bf16),
            pltpu.VMEM((units, BLOCK, width), bf16),
            pltpu.SMEM((segs, homes), jnp.int32),
            dma,
            dma((3, units)),
            dma((4, units)),
            dma((4, units)),
            dma,
            dma,
            dma((units,)),
            dma,
            dma((units,)),
            dma,
        ],
        compiler_params=pltpu.CompilerParams(
            collective_id=0, has_side_effects=True, vmem_limit_bytes=12 * 1024 * 1024
        ),
        cost_estimate=pl.CostEstimate(
            flops=4 * rows * WINDOW * feats,
            bytes_accessed=8 * rows * feats,
            transcendentals=rows * WINDOW * heads,
        ),
        name="segment_attention",
    )(*(pltpu.with_memory_space_constraint(x, pltpu.HBM) for x in (jnp.swapaxes(seg_len, 1, 2), queries, keys, values)))
    return handed[None]


def solution(mesh):
    sections, homes = mesh.shape["section"], mesh.shape["pack"]
    return jax.shard_map(
        functools.partial(per_device, sections, homes),
        mesh=mesh,
        in_specs=(
            P("section", "pack", "tensor"),
            P("section", "pack", "tensor"),
            P("section", "pack", "tensor"),
            P(),
        ),
        out_specs=P("section", ("pack", "tensor"), None),
        check_vma=False,
    )
```

time: 40.6 us -> 29.7 us (0.73)
  the two profiles are of different devices: /device:TPU:1 before, /device:TPU:161 now
where the time goes in v2:
time: 29.7 us; the launch traced here: 29.6 us
  Pallas kernels  28.5 us (96%)
  local copies, waits for them, and re-layouts  1.06 us (4%)
    pallas_call x1, Pallas kernels, per_device(): pl.pallas_call(functools.partial(kernel, (sections, homes, heads, rows, s...  28.5 us
    unnamed x1, local copies, waits for them, and re-layouts  1.06 us

profile of v2, /device:TPU:161, one launch (start us, length us, event | category | flops | bytes accessed | tf_op | source)
XLA Modules:
  0.0 29.6 jit_solution(1016466251215332656)
XLA Ops:
  0.0 28.5 %segment_attention.1 = bf16[256,2560]{1,0:T(8,128)(2,1)S(1)} custom-call(s32[4,16,32]{2,1,0:T(8,128)} %bitcast.3, bf16[1,512,1280]{2,1,0:T(8,128)(2,1)} %q_hbm.1, bf16[1,512,1280]{2,1,0:T(8,128)(2,1)} %k_hbm.1, bf16[1,512,1280]{2,1,0:T(8,128)(2,1)} %v_hbm.1), custom_call_target="tpu_custom_call" | custom-call | flops 671088640 | bytes 5242880 | tf_op jit(solution)/shard_map/segment_attention/pallas_call | solution.py:285
  28.5 1.1 %copy.6 = bf16[1,256,2560]{2,1,0:T(8,128)(2,1)} copy(bf16[1,256,2560]{2,1,0:T(8,128)(2,1)S(1)} %bitcast.2) | data formatting | bytes 2621440

commit v3 on v2

--- a/solution.py
+++ b/solution.py
@@ -15,6 +15,7 @@
 MESH = pl.DeviceIdType.MESH
 MASKED = -3.0e38
 GROUP = 2
+ROW = 4
 
 
 def kernel(
@@ -31,6 +32,10 @@
     stage,
     relay_one,
     relay_two,
+    extra,
+    extra_recv,
+    extra_send,
+    ready,
     len_ref,
     len_sem,
     load_sem,
@@ -49,8 +54,9 @@
     ahead, behind = lax.rem(s + 1, sections), lax.rem(s + sections - 1, sections)
     after, before = lax.rem(p + 1, homes), lax.rem(p + homes - 1, homes)
 
+    has_after, has_before = p < homes - 1, p > 0
+
     barrier = pltpu.get_barrier_semaphore()
-    has_after, has_before = p < homes - 1, p > 0
 
     def greet(partner):
         pl.semaphore_signal(barrier, inc=1, device_id=partner, device_id_type=MESH)
@@ -59,7 +65,10 @@
     for partner in partners:
         greet(partner)
 
-    @pl.when(has_after)
+    far_after = (p >= homes // 2) & (lax.rem(p, ROW) == ROW - 1) & has_after
+    far_before = (p > homes // 2) & (lax.rem(p, ROW) == 0)
+
+    @pl.when(has_after & jnp.logical_not(far_after))
     def _():
         greet((s, after, t))
 
@@ -151,113 +160,196 @@
 
     factor = math.log2(math.e) / math.sqrt(HEAD_DIM)
 
-    def attend(b, u):
-        for g in range(GROUP):
-            cols = pl.ds(pl.multiple_of(u * width, width) + g * HEAD_DIM, HEAD_DIM)
-            scores = lax.dot_general(
-                q_buf[b * BLOCK : (b + 1) * BLOCK, cols],
-                k_buf[b * BLOCK : b * BLOCK + WINDOW, cols],
-                (((1,), (1,)), ((), ())),
-                preferred_element_type=jnp.float32,
-            )
-            scores = scores + bias[b]
-            row_max = jnp.max(scores, axis=1, keepdims=True)
-            weights = jnp.exp2((scores - row_max) * factor)
-            weights = weights * (1.0 / jnp.sum(weights, axis=1, keepdims=True))
-            mixed = jnp.dot(
-                weights.astype(jnp.bfloat16),
-                v_buf[b * BLOCK : b * BLOCK + WINDOW, cols],
-                preferred_element_type=jnp.float32,
-            )
-            stage[b, u, :, g * HEAD_DIM : (g + 1) * HEAD_DIM] = mixed.astype(jnp.bfloat16)
+    def attend(b, h):
+        cols = pl.ds(pl.multiple_of(h * HEAD_DIM, HEAD_DIM), HEAD_DIM)
+        scores = lax.dot_general(
+            q_buf[b * BLOCK : (b + 1) * BLOCK, cols],
+            k_buf[b * BLOCK : b * BLOCK + WINDOW, cols],
+            (((1,), (1,)), ((), ())),
+            preferred_element_type=jnp.float32,
+        )
+        scores = scores + bias[b]
+        row_max = jnp.max(scores, axis=1, keepdims=True)
+        weights = jnp.exp2((scores - row_max) * factor)
+        weights = weights * (1.0 / jnp.sum(weights, axis=1, keepdims=True))
+        mixed = jnp.dot(
+            weights.astype(jnp.bfloat16),
+            v_buf[b * BLOCK : b * BLOCK + WINDOW, cols],
+            preferred_element_type=jnp.float32,
+        )
+        stage[b, :, cols] = mixed.astype(jnp.bfloat16)
 
     def final_place(b, u):
         start = pl.multiple_of(t * feats + u * width, HEAD_DIM)
         return out_ref.at[pl.ds((b % 2) * BLOCK, BLOCK), pl.ds(start, width)]
 
-    def forward(b, u):
+    def copy_to(source, target, send, recv, device):
         return pltpu.make_async_remote_copy(
-            src_ref=stage.at[b, u],
-            dst_ref=final_place(b, u),
-            send_sem=out_send,
-            recv_sem=out_recv,
-            device_id=(ahead, p, b // 2),
+            src_ref=source,
+            dst_ref=target,
+            send_sem=send,
+            recv_sem=recv,
+            device_id=device,
             device_id_type=MESH,
         )
 
+    def forward(b, u):
+        source = stage.at[b, :, unit_cols(u)]
+        return copy_to(source, final_place(b, u), out_send, out_recv, (ahead, p, b // 2))
+
     def hop_one(u):
-        return pltpu.make_async_remote_copy(
-            src_ref=stage.at[1, u],
-            dst_ref=relay_one.at[u],
-            send_sem=out_send,
-            recv_sem=one_recv.at[u],
-            device_id=(behind, p, t),
-            device_id_type=MESH,
-        )
+        cols = unit_cols(u)
+        return copy_to(stage.at[1, :, cols], relay_one.at[:, cols], out_send, one_recv.at[u], (behind, p, t))
 
     def hop_two(u):
-        return pltpu.make_async_remote_copy(
-            src_ref=relay_one.at[u],
-            dst_ref=relay_two.at[u],
-            send_sem=one_send,
-            recv_sem=two_recv.at[u],
-            device_id=(behind, p, t),
-            device_id_type=MESH,
-        )
+        cols = unit_cols(u)
+        return copy_to(relay_one.at[:, cols], relay_two.at[:, cols], one_send, two_recv.at[u], (behind, p, t))
 
     def hop_three(u):
-        return pltpu.make_async_remote_copy(
-            src_ref=relay_two.at[u],
-            dst_ref=final_place(1, u),
-            send_sem=two_send,
-            recv_sem=out_recv,
-            device_id=(behind, p, 0),
-            device_id_type=MESH,
-        )
+        source = relay_two.at[:, unit_cols(u)]
+        return copy_to(source, final_place(1, u), two_send, out_recv, (behind, p, 0))
+
+    def make(u, blocks):
+        for g in range(GROUP):
+            for b in blocks:
+                attend(b, u * GROUP + g)
 
     def make_inner(u):
         for load in loads(u):
             load.wait()
-        attend(1, u)
-        attend(2, u)
+        make(u, (1, 2))
 
     def send_inner(u):
         hop_one(u).start()
         forward(2, u).start()
-        each_side(lambda side: [copy.start() for copy in halo(u, side)], (has_after, has_before))
+
+    def start_halos(conditions):
+        def start_halo(u, carry):
+            each_side(lambda side: [copy.start() for copy in halo(u, side)], conditions)
+            return carry
+
+        lax.fori_loop(0, units, start_halo, 0)
 
     make_inner(0)
 
-    pack_peers = jnp.where(has_after, 1, 0) + jnp.where(has_before, 1, 0)
+    pack_peers = jnp.where(has_after, 1, 0) + jnp.where(has_before & jnp.logical_not(far_before), 1, 0)
     pl.semaphore_wait(barrier, len(partners) + pack_peers)
 
+    @pl.when(far_after)
+    def _():
+        pl.semaphore_signal(ready, inc=1, device_id=(s, after, t), device_id_type=MESH)
+
+    send_inner(0)
+    start_halos((has_after, has_before & jnp.logical_not(far_before)))
+
     def inner(u, carry):
-        send_inner(u - 1)
         make_inner(u)
+        send_inner(u)
         return carry
 
-    lax.fori_loop(1, units, inner, 0)
-    send_inner(units - 1)
-
-    def outer(u, carry):
-        each_side(lambda side: [copy.wait_recv() for copy in halo(u, side)], (has_before, has_after))
-        attend(0, u)
-        attend(3, u)
-        forward(0, u).start()
-        forward(3, u).start()
-        hop_one(u).wait_recv()
-        hop_two(u).start()
-        return carry
-
-    lax.fori_loop(0, units, outer, 0)
+    lax.fori_loop(1, units - 1, inner, 0)
+
+    end_cols = pl.ds(feats - HEAD_DIM, HEAD_DIM)
+    extra_one = copy_to(stage.at[2, :, end_cols], extra.at[0], out_send, extra_recv.at[0], (behind, p, t))
+    extra_two = copy_to(extra.at[0], extra.at[1], extra_send.at[0], extra_recv.at[1], (behind, p, t))
+    extra_start = pl.multiple_of(t * feats + feats - HEAD_DIM, HEAD_DIM)
+    extra_place = out_ref.at[pl.ds(0, BLOCK), pl.ds(extra_start, HEAD_DIM)]
+    extra_three = copy_to(extra.at[1], extra_place, extra_send.at[1], out_recv, (behind, p, 1))
+    is_last = s == sections - 1
+
+    make_inner(units - 1)
+    hop_one(units - 1).start()
+
+    @pl.when(jnp.logical_not(is_last))
+    def _():
+        forward(2, units - 1).start()
+
+    @pl.when(is_last)
+    def _():
+        part_start = (units - 1) * width
+        part_place = out_ref.at[
+            pl.ds(0, BLOCK), pl.ds(pl.multiple_of(t * feats + part_start, HEAD_DIM), width - HEAD_DIM)
+        ]
+        part = stage.at[2, :, pl.ds(part_start, width - HEAD_DIM)]
+        extra_one.start()
+        copy_to(part, part_place, out_send, out_recv, (ahead, p, 1)).start()
+
+    @pl.when(far_before)
+    def _():
+        pl.semaphore_wait(ready, 1)
+
+        def start_before(u, carry):
+            for copy in halo(u, 1):
+                copy.start()
+            return carry
+
+        lax.fori_loop(0, units, start_before, 0)
+
+    def outer(b, relays):
+        side, exists = (0, has_before) if b == 0 else (1, has_after)
+
+        def step(u, carry):
+            @pl.when(exists)
+            def _():
+                for copy in halo(u, side):
+                    copy.wait_recv()
+
+            make(u, (b,))
+            forward(b, u).start()
+            if relays:
+                hop_one(u).wait_recv()
+                hop_two(u).start()
+            return carry
+
+        lax.fori_loop(0, units, step, 0)
+
+    def both_outer(first, second):
+        outer(first, True)
+
+        @pl.when(s == sections - 2)
+        def _():
+            extra_one.wait_recv()
+            extra_two.start()
+
+        outer(second, False)
+
+    row_end = lax.rem(p, ROW) == ROW - 1
+
+    @pl.when(jnp.logical_not(row_end))
+    def _():
+        both_outer(3, 0)
+
+    @pl.when(row_end)
+    def _():
+        both_outer(0, 3)
 
     def last(u, carry):
         hop_two(u).wait_recv()
         hop_three(u).start()
+        return carry
+
+    lax.fori_loop(0, units - 2, last, 0)
+
+    @pl.when(s == sections - 3)
+    def _():
+        extra_two.wait_recv()
+        extra_three.start()
+
+    lax.fori_loop(units - 2, units, last, 0)
+
+    @pl.when(s == sections - 3)
+    def _():
+        extra_three.wait_send()
+
+    @pl.when(s == sections - 2)
+    def _():
+        extra_two.wait_send()
+
+    def end_halo(u, carry):
         each_side(lambda side: [copy.wait_send() for copy in halo(u, side)], (has_after, has_before))
         return carry
 
-    lax.fori_loop(0, units, last, 0)
+    lax.fori_loop(0, units, end_halo, 0)
 
     def whole(ref, send, recv):
         return pltpu.make_async_remote_copy(
@@ -269,7 +361,7 @@
             device_id_type=MESH,
         )
 
-    whole(stage, out_send, out_recv).wait_send()
+    whole(out_ref, out_send, out_recv).wait_send()
     whole(relay_one, one_send, out_recv).wait_send()
     whole(relay_two, two_send, out_recv).wait_send()
     whole(out_ref, out_send, out_recv).wait_recv()
@@ -279,7 +371,7 @@
     _, rows, feats = queries.shape
     heads = feats // HEAD_DIM
     segs = seg_len.shape[2]
-    blocks, units, width = rows // BLOCK, heads // GROUP, GROUP * HEAD_DIM
+    blocks, units = rows // BLOCK, heads // GROUP
     bf16 = jnp.bfloat16
     dma = pltpu.SemaphoreType.DMA
     handed = pl.pallas_call(
@@ -292,9 +384,13 @@
             pltpu.VMEM((rows + 2 * HALO, feats), bf16),
             pltpu.VMEM((rows + 2 * HALO, feats), bf16),
             pltpu.VMEM((blocks, BLOCK, WINDOW), jnp.float32),
-            pltpu.VMEM((blocks, units, BLOCK, width), bf16),
-            pltpu.VMEM((units, BLOCK, width), bf16),
-            pltpu.VMEM((units, BLOCK, width), bf16),
+            pltpu.VMEM((blocks, BLOCK, feats), bf16),
+            pltpu.VMEM((BLOCK, feats), bf16),
+            pltpu.VMEM((BLOCK, feats), bf16),
+            pltpu.VMEM((2, BLOCK, HEAD_DIM), bf16),
+            dma((2,)),
+            dma((2,)),
+            pltpu.SemaphoreType.REGULAR,
             pltpu.SMEM((segs, homes), jnp.int32),
             dma,
             dma((3, units)),

time: 29.7 us -> 28.5 us (0.960)
  the two profiles are of different devices: /device:TPU:161 before, /device:TPU:24 now
where the time goes in v3:
time: 28.5 us; the launch traced here: 28 us
  Pallas kernels  27 us (95%)
  local copies, waits for them, and re-layouts  1.06 us (4%)
    pallas_call x1, Pallas kernels, per_device(): pl.pallas_call(functools.partial(kernel, (sections, homes, heads, rows, s...  27 us
    unnamed x1, local copies, waits for them, and re-layouts  1.06 us

profile of v3, /device:TPU:24, one launch (start us, length us, event | category | flops | bytes accessed | tf_op | source)
XLA Modules:
  0.0 28.0 jit_solution(11594123050177965849)
XLA Ops:
  0.0 27.0 %segment_attention.1 = bf16[256,2560]{1,0:T(8,128)(2,1)S(1)} custom-call(s32[4,16,32]{2,1,0:T(8,128)} %bitcast.3, bf16[1,512,1280]{2,1,0:T(8,128)(2,1)} %q_hbm.1, bf16[1,512,1280]{2,1,0:T(8,128)(2,1)} %k_hbm.1, bf16[1,512,1280]{2,1,0:T(8,128)(2,1)} %v_hbm.1), custom_call_target="tpu_custom_call" | custom-call | flops 671088640 | bytes 5242880 | tf_op jit(solution)/shard_map/segment_attention/pallas_call | solution.py:377
  27.0 1.1 %copy.6 = bf16[1,256,2560]{2,1,0:T(8,128)(2,1)} copy(bf16[1,256,2560]{2,1,0:T(8,128)(2,1)S(1)} %bitcast.2) | data formatting | bytes 2621440

commit v4 on v3

--- a/solution.py
+++ b/solution.py
@@ -65,19 +65,19 @@
     for partner in partners:
         greet(partner)
 
-    far_after = (p >= homes // 2) & (lax.rem(p, ROW) == ROW - 1) & has_after
-    far_before = (p > homes // 2) & (lax.rem(p, ROW) == 0)
+    mid_after, mid_before = p == homes // 2 - 1, p == homes // 2
+    far_after = (lax.rem(p, ROW) == ROW - 1) & has_after & jnp.logical_not(mid_after)
+    far_before = (lax.rem(p, ROW) == 0) & has_before & jnp.logical_not(mid_before)
+    near_after = has_after & jnp.logical_not(mid_after)
+    near_before = has_before & jnp.logical_not(far_before)
 
     @pl.when(has_after & jnp.logical_not(far_after))
     def _():
         greet((s, after, t))
 
-    @pl.when(has_before)
+    @pl.when(has_before & jnp.logical_not(mid_before))
     def _():
         greet((s, before, t))
-
-    fetch_lengths = pltpu.make_async_copy(len_hbm.at[s], len_ref, len_sem)
-    fetch_lengths.start()
 
     units = heads // GROUP
     width = GROUP * HEAD_DIM
@@ -98,7 +98,9 @@
             load.start()
         return carry
 
-    lax.fori_loop(0, units, start_loads, 0)
+    fetch_lengths = pltpu.make_async_copy(len_hbm.at[s], len_ref, len_sem)
+    start_loads(0, 0)
+    fetch_lengths.start()
 
     @pl.when(jnp.logical_not(has_before))
     def _():
@@ -126,12 +128,15 @@
         return total
 
     key_label = labels(lax.broadcasted_iota(jnp.int32, (8, rows + 2 * HALO), 1) - HALO)
-    for b in range(rows // BLOCK):
+    def make_bias(b):
         query_label = labels(lax.broadcasted_iota(jnp.int32, (BLOCK, 128), 0) + b * BLOCK)
         for c in range(WINDOW // 128):
             start = b * BLOCK + c * 128
             same = query_label == key_label[0:1, start : start + 128]
             bias[b, :, c * 128 : c * 128 + 128] = jnp.where(same, 0.0, MASKED)
+
+    make_bias(1)
+    make_bias(2)
 
     def halo(u, side):
         cols = unit_cols(u)
@@ -160,25 +165,6 @@
 
     factor = math.log2(math.e) / math.sqrt(HEAD_DIM)
 
-    def attend(b, h):
-        cols = pl.ds(pl.multiple_of(h * HEAD_DIM, HEAD_DIM), HEAD_DIM)
-        scores = lax.dot_general(
-            q_buf[b * BLOCK : (b + 1) * BLOCK, cols],
-            k_buf[b * BLOCK : b * BLOCK + WINDOW, cols],
-            (((1,), (1,)), ((), ())),
-            preferred_element_type=jnp.float32,
-        )
-        scores = scores + bias[b]
-        row_max = jnp.max(scores, axis=1, keepdims=True)
-        weights = jnp.exp2((scores - row_max) * factor)
-        weights = weights * (1.0 / jnp.sum(weights, axis=1, keepdims=True))
-        mixed = jnp.dot(
-            weights.astype(jnp.bfloat16),
-            v_buf[b * BLOCK : b * BLOCK + WINDOW, cols],
-            preferred_element_type=jnp.float32,
-        )
-        stage[b, :, cols] = mixed.astype(jnp.bfloat16)
-
     def final_place(b, u):
         start = pl.multiple_of(t * feats + u * width, HEAD_DIM)
         return out_ref.at[pl.ds((b % 2) * BLOCK, BLOCK), pl.ds(start, width)]
@@ -210,9 +196,31 @@
         return copy_to(source, final_place(1, u), two_send, out_recv, (behind, p, 0))
 
     def make(u, blocks):
-        for g in range(GROUP):
-            for b in blocks:
-                attend(b, u * GROUP + g)
+        places = [
+            (b, pl.ds(pl.multiple_of(u * width, width) + g * HEAD_DIM, HEAD_DIM))
+            for g in range(GROUP)
+            for b in blocks
+        ]
+        scores = [
+            lax.dot_general(
+                q_buf[b * BLOCK : (b + 1) * BLOCK, cols],
+                k_buf[b * BLOCK : b * BLOCK + WINDOW, cols],
+                (((1,), (1,)), ((), ())),
+                preferred_element_type=jnp.float32,
+            )
+            + bias[b]
+            for b, cols in places
+        ]
+        maxima = [jnp.max(score, axis=1, keepdims=True) for score in scores]
+        weights = [jnp.exp2((score - top) * factor) for score, top in zip(scores, maxima)]
+        sums = [jnp.sum(weight, axis=1, keepdims=True) for weight in weights]
+        weights = [(weight * (1.0 / total)).astype(jnp.bfloat16) for weight, total in zip(weights, sums)]
+        mixed = [
+            jnp.dot(weight, v_buf[b * BLOCK : b * BLOCK + WINDOW, cols], preferred_element_type=jnp.float32)
+            for weight, (b, cols) in zip(weights, places)
+        ]
+        for value, (b, cols) in zip(mixed, places):
+            stage[b, :, cols] = value.astype(jnp.bfloat16)
 
     def make_inner(u):
         for load in loads(u):
@@ -230,17 +238,24 @@
 
         lax.fori_loop(0, units, start_halo, 0)
 
-    make_inner(0)
-
-    pack_peers = jnp.where(has_after, 1, 0) + jnp.where(has_before & jnp.logical_not(far_before), 1, 0)
+    for load in loads(0):
+        load.wait()
+    lax.fori_loop(1, units, start_loads, 0)
+    make(0, (1, 2))
+
+    pack_peers = jnp.where(near_after, 1, 0) + jnp.where(near_before, 1, 0)
     pl.semaphore_wait(barrier, len(partners) + pack_peers)
 
     @pl.when(far_after)
     def _():
         pl.semaphore_signal(ready, inc=1, device_id=(s, after, t), device_id_type=MESH)
 
+    @pl.when(mid_before)
+    def _():
+        pl.semaphore_signal(ready, inc=1, device_id=(s, before, t), device_id_type=MESH)
+
     send_inner(0)
-    start_halos((has_after, has_before & jnp.logical_not(far_before)))
+    start_halos((near_after, near_before))
 
     def inner(u, carry):
         make_inner(u)
@@ -274,16 +289,13 @@
         extra_one.start()
         copy_to(part, part_place, out_send, out_recv, (ahead, p, 1)).start()
 
-    @pl.when(far_before)
+    make_bias(0)
+    make_bias(3)
+
+    @pl.when(far_before | mid_after)
     def _():
         pl.semaphore_wait(ready, 1)
-
-        def start_before(u, carry):
-            for copy in halo(u, 1):
-                copy.start()
-            return carry
-
-        lax.fori_loop(0, units, start_before, 0)
+        start_halos((mid_after, far_before))
 
     def outer(b, relays):
         side, exists = (0, has_before) if b == 0 else (1, has_after)
@@ -295,13 +307,23 @@
                     copy.wait_recv()
 
             make(u, (b,))
-            forward(b, u).start()
             if relays:
+                forward(b, u).start()
                 hop_one(u).wait_recv()
                 hop_two(u).start()
             return carry
 
-        lax.fori_loop(0, units, step, 0)
+        if relays:
+            lax.fori_loop(0, units, step, 0)
+        else:
+            for first, end in ((0, 2), (2, units)):
+                lax.fori_loop(first, end, step, 0)
+                cols = pl.ds(first * width, (end - first) * width)
+                start = pl.multiple_of(t * feats + first * width, HEAD_DIM)
+                place = out_ref.at[
+                    pl.ds((b % 2) * BLOCK, BLOCK), pl.ds(start, (end - first) * width)
+                ]
+                copy_to(stage.at[b, :, cols], place, out_send, out_recv, (ahead, p, b // 2)).start()
 
     def both_outer(first, second):
         outer(first, True)

time: 28.5 us -> 28.1 us (0.986)
  Pallas kernels: 27 us -> 26.6 us
    pallas_call x1, Pallas kernels: 27 us -> 26.6 us  [per_device(): pl.pallas_call(functools.partial(kernel, (sections, homes, heads, rows, s...]
where the time goes in v4:
time: 28.1 us; the launch traced here: 27.6 us
  Pallas kernels  26.6 us (95%)
  local copies, waits for them, and re-layouts  1.06 us (4%)
    pallas_call x1, Pallas kernels, per_device(): pl.pallas_call(functools.partial(kernel, (sections, homes, heads, rows, s...  26.6 us
    unnamed x1, local copies, waits for them, and re-layouts  1.06 us

profile of v4, /device:TPU:24, one launch (start us, length us, event | category | flops | bytes accessed | tf_op | source)
XLA Modules:
  0.0 27.6 jit_solution(11374317616506260986)
XLA Ops:
  0.0 26.6 %segment_attention.1 = bf16[256,2560]{1,0:T(8,128)(2,1)S(1)} custom-call(s32[4,16,32]{2,1,0:T(8,128)} %bitcast.3, bf16[1,512,1280]{2,1,0:T(8,128)(2,1)} %q_hbm.1, bf16[1,512,1280]{2,1,0:T(8,128)(2,1)} %k_hbm.1, bf16[1,512,1280]{2,1,0:T(8,128)(2,1)} %v_hbm.1), custom_call_target="tpu_custom_call" | custom-call | flops 671088640 | bytes 5242880 | tf_op jit(solution)/shard_map/segment_attention/pallas_call | solution.py:399
  26.6 1.1 %copy.6 = bf16[1,256,2560]{2,1,0:T(8,128)(2,1)} copy(bf16[1,256,2560]{2,1,0:T(8,128)(2,1)S(1)} %bitcast.2) | data formatting | bytes 2621440

commit v5 on v4

--- a/solution.py
+++ b/solution.py
@@ -183,6 +183,12 @@
         source = stage.at[b, :, unit_cols(u)]
         return copy_to(source, final_place(b, u), out_send, out_recv, (ahead, p, b // 2))
 
+    def forward_heads(b, first, count):
+        cols = pl.ds(pl.multiple_of(first * HEAD_DIM, HEAD_DIM), count * HEAD_DIM)
+        start = pl.multiple_of(t * feats + first * HEAD_DIM, HEAD_DIM)
+        place = out_ref.at[pl.ds((b % 2) * BLOCK, BLOCK), pl.ds(start, count * HEAD_DIM)]
+        return copy_to(stage.at[b, :, cols], place, out_send, out_recv, (ahead, p, b // 2))
+
     def hop_one(u):
         cols = unit_cols(u)
         return copy_to(stage.at[1, :, cols], relay_one.at[:, cols], out_send, one_recv.at[u], (behind, p, t))
@@ -308,7 +314,15 @@
 
             make(u, (b,))
             if relays:
-                forward(b, u).start()
+
+                @pl.when(lax.rem(u, 2) == 1)
+                def _():
+                    forward_heads(b, (u - 1) * GROUP, 2 * GROUP).start()
+
+                @pl.when(u == units - 1)
+                def _():
+                    forward(b, u).start()
+
                 hop_one(u).wait_recv()
                 hop_two(u).start()
             return carry
@@ -316,14 +330,11 @@
         if relays:
             lax.fori_loop(0, units, step, 0)
         else:
-            for first, end in ((0, 2), (2, units)):
+            first = 0
+            for end in (units,):
                 lax.fori_loop(first, end, step, 0)
-                cols = pl.ds(first * width, (end - first) * width)
-                start = pl.multiple_of(t * feats + first * width, HEAD_DIM)
-                place = out_ref.at[
-                    pl.ds((b % 2) * BLOCK, BLOCK), pl.ds(start, (end - first) * width)
-                ]
-                copy_to(stage.at[b, :, cols], place, out_send, out_recv, (ahead, p, b // 2)).start()
+                forward_heads(b, first * GROUP, (end - first) * GROUP).start()
+                first = end
 
     def both_outer(first, second):
         outer(first, True)

time: 28.1 us -> 28.1 us (level)
  no operation moved by 1% of the time
where the time goes in v5:
time: 28.1 us; the launch traced here: 27.6 us
  Pallas kernels  26.6 us (95%)
  local copies, waits for them, and re-layouts  1.06 us (4%)
    pallas_call x1, Pallas kernels, per_device(): pl.pallas_call(functools.partial(kernel, (sections, homes, heads, rows, s...  26.6 us
    unnamed x1, local copies, waits for them, and re-layouts  1.06 us

profile of v5, /device:TPU:24, one launch (start us, length us, event | category | flops | bytes accessed | tf_op | source)
XLA Modules:
  0.0 27.6 jit_solution(3489723914076437621)
XLA Ops:
  0.0 26.6 %segment_attention.1 = bf16[256,2560]{1,0:T(8,128)(2,1)S(1)} custom-call(s32[4,16,32]{2,1,0:T(8,128)} %bitcast.3, bf16[1,512,1280]{2,1,0:T(8,128)(2,1)} %q_hbm.1, bf16[1,512,1280]{2,1,0:T(8,128)(2,1)} %k_hbm.1, bf16[1,512,1280]{2,1,0:T(8,128)(2,1)} %v_hbm.1), custom_call_target="tpu_custom_call" | custom-call | flops 671088640 | bytes 5242880 | tf_op jit(solution)/shard_map/segment_attention/pallas_call | solution.py:410
  26.6 1.1 %copy.6 = bf16[1,256,2560]{2,1,0:T(8,128)(2,1)} copy(bf16[1,256,2560]{2,1,0:T(8,128)(2,1)S(1)} %bitcast.2) | data formatting | bytes 2621440
